TPU v7x, 32 devices: a whole 2x2x4 slice. The times are simulated.
32 devices in a mesh: grp: 2 (over y), doc: 8 (over z, x), layer: 2 (over core).
Axes of the slice: x: 2, y: 2, z: 4, core: 2. Of those that a mesh axis runs over, the one named last changes fastest.
Arguments:
- query_grads: bfloat16 [2048, 2, 4096], P(('grp', 'doc'), 'layer'), parts along dimension 0, may hold values from -6 to 6
- doc_grads: bfloat16 [6144, 2, 4096], P(('grp', 'doc'), 'layer'), parts along dimension 0, may hold values from -0.0625 to 0.0625
- query_ids: int32 [2048], P('grp'), parts along dimension 0, may hold values from 0 to 3071
- doc_ids: int32 [6144], P(('grp', 'doc')), parts along dimension 0, may hold values from 0 to 3071, each once
Outputs:
- scores: float32 [2048, 3072], P('grp', ('doc', 'layer')), parts along dimension 0
There are 2 independent parts, one for each index of `grp`. A program takes and returns all parts, laid end to end along the dimension named above; each array names one. Nothing has to cross between parts.
Inputs may be any that keep to these rules, and one draw needn't show every extreme that they name: doc_ids names every document number once.
All inputs are finite; a program needn't handle non-finite values.
Results may differ from a plain program's by a relative error of at most 0.0003.
Values may be sent and summed in bfloat16 or wider, within the bound.
A program may use at most 64 MiB of HBM per device.

v0:
```python
import jax
import jax.numpy as jnp
from jax import lax
from jax.sharding import PartitionSpec as P


def on_device(query_grads, doc_grads, query_ids, doc_ids):
    queries = query_grads.reshape(query_grads.shape[0], -1)
    documents = doc_grads.reshape(doc_grads.shape[0], -1)
    every = lax.all_gather(queries, "doc", axis=0, tiled=True)
    raw = lax.dot_general(
        every, documents, (((1,), (1,)), ((), ())), preferred_element_type=jnp.float32
    )
    same = query_ids[:, None] == doc_ids[None, :]
    partial_scores = jnp.where(same, jnp.zeros_like(raw), raw)
    return lax.psum_scatter(partial_scores, "layer", scatter_dimension=1, tiled=True)


def solution(mesh):
    in_specs = (
        P(("grp", "doc"), "layer", None),
        P(("grp", "doc"), "layer", None),
        P("grp"),
        P(("grp", "doc")),
    )
    out_specs = P("grp", ("doc", "layer"))
    return jax.shard_map(
        on_device, mesh=mesh, in_specs=in_specs, out_specs=out_specs, check_vma=False
    )
```

profile of v0, /device:TPU:0, one launch (start us, length us, event | category | flops | bytes accessed | tf_op | source)
XLA Modules:
  0.0 159.5 jit_solution(6099552106978484111)
XLA Ops:
  6.5 0.0 copy-start
  6.5 0.0 all-gather.3.cloned.1.call-start
  6.5 0.7 all-gather.3.cloned.1.call-update
  7.3 0.0 reduce-scatter.2.cloned.1.call-start
  7.3 129.8 %all-gather.3.cloned.1.call-done = bf16[1024,1,4096]{2,0,1:T(8,128)(2,1)} async-done(((bf16[128,1,4096]{2,0,1:T(8,128)(2,1)}), bf16[1024,1,4096]{2,0,1:T(8,128)(2,1)}) %all-gather.3.cloned.1.call-update) | async-done | bytes 8388624 | tf_op jit(solution)/shard_map/all_gather | solution.py:10
  137.1 0.0 copy-done
  137.1 8.1 %compare_select_fusion = f32[1024,384]{0,1:T(8,128)} fusion(bf16[384,1,4096]{2,0,1:T(8,128)(2,1)S(1)} %copy-done, bf16[1024,1,4096]{2,0,1:T(8,128)(2,1)} %all-gather.3.cloned.1.call-done, s32[1024]{0:T(1024)} %param.6, s32[384]{0:T(512)} %param.7), kind=kOutput, calls=%fused_computation.3 | convolution fusion | flops 3222011904 | bytes 13112832 | tf_op jit(solution)/shard_map/dot_general | solution.py:11
  145.2 0.0 reduce-scatter.2.cloned.1.call-update
  145.2 7.4 %reduce-scatter.2.cloned.1.call-done = f32[1024,192]{0,1:T(8,128)} async-done(((f32[1024,384]{0,1:T(8,128)}), f32[1024,192]{0,1:T(8,128)}) %reduce-scatter.2.cloned.1.call-update) | async-done | bytes 786448 | tf_op jit(solution)/shard_map/reduce_scatter | solution.py:16
Async XLA Ops:
  6.5 130.6 %copy-start = (bf16[384,1,4096]{2,0,1:T(8,128)(2,1)S(1)}, bf16[384,1,4096]{2,0,1:T(8,128)(2,1)}, u32[]{:S(2)}) copy-start(bf16[384,1,4096]{2,0,1:T(8,128)(2,1)} %param.5) | copy-start | bytes 9437188
  6.5 130.6 %all-gather.3.cloned.1.call-start = ((), (), s32[]{:S(2)}) async-start(), calls=%async_computation.2 | async-start | bytes 9437184 | tf_op jit(solution)/shard_map/all_gather | solution.py:10
  7.3 145.4 %reduce-scatter.2.cloned.1.call-start = ((), (), s32[]{:S(2)}) async-start(), calls=%async_computation.1 | async-start | bytes 2359296 | tf_op jit(solution)/shard_map/reduce_scatter | solution.py:16
Sparse Core Ops, SparseCore 0:
  9.5 127.6 all-gather.2
  145.4 7.2 reduce-scatter.1
where the time goes:
time: 160 us; the launch traced here: 159 us
  waiting for transfers between devices  138 us (86%)
  between operations  13.4 us (8%)
  matrix products  8.06 us (5%)
    all_gather x1, waiting for transfers between devices, on_device(): every = lax.all_gather(queries, 'doc', axis=0, tiled=True)  130 us
    dot_general x1, matrix products, on_device(): lax.dot_general(every, documents, (((1,), (1,)), ((), ())), preferred_ele...  8.06 us
    reduce_scatter x1, waiting for transfers between devices, on_device(): lax.psum_scatter(partial_scores, 'layer', scatter_dimension=1, tiled=True)  7.4 us
  transfers between devices with their start and end apart: 2, of which 2 were waited for; matrix products, arithmetic and copies ran while one was open for 0% of the time, Pallas kernels for 0%

commit v1 on v0

v1 whole, which is shorter than its diff:
```python
import functools

import jax
import jax.numpy as jnp
from jax import lax
from jax.experimental import pallas as pl
from jax.experimental.pallas import tpu as pltpu
from jax.sharding import PartitionSpec as P

MESH = pl.DeviceIdType.MESH
NT = (((1,), (1,)), ((), ()))


def kernel(
    nz, q_ref, d_ref, o_ref, Q, D, CS, CR, ACC, XR,
    loc, xq_s, xq_r, xd_s, xd_r, up_s, up_r, dn_s, dn_r, c_s, c_r, o_s, o_r,
):
    g, d, c = lax.axis_index("grp"), lax.axis_index("doc"), lax.axis_index("layer")
    z, x = d // 2, d % 2
    partner, other = (g, d + 1 - 2 * x, c), (g, d, 1 - c)
    above, below = (g, d + 2, c), (g, d - 2, c)
    has_above, has_below = z < nz - 1, z > 0
    rows, half = Q.shape[2], Q.shape[3]
    ch = rows // 2
    nd = D.shape[1] // 2
    dch = D.shape[1] // xd_s.shape[0]
    mine = pl.multiple_of(x * half, half)
    theirs = pl.multiple_of((1 - x) * half, half)

    barrier = pltpu.get_barrier_semaphore()

    def greet(device):
        pl.semaphore_signal(barrier, inc=1, device_id=device, device_id_type=MESH)

    greet(partner)
    greet(other)

    @pl.when(has_above)
    def _():
        greet(above)

    @pl.when(has_below)
    def _():
        greet(below)

    own_q = pltpu.make_async_copy(q_ref.at[:, pl.ds(mine, half)], Q.at[z, 0], loc.at[0])
    own_d = pltpu.make_async_copy(d_ref.at[:, pl.ds(mine, half)], D.at[0], loc.at[1])
    own_q.start()
    own_d.start()
    pl.semaphore_wait(barrier, 2 + jnp.where(has_above, 1, 0) + jnp.where(has_below, 1, 0))

    def remote(src, dst, ss, rs, device):
        return pltpu.make_async_remote_copy(
            src_ref=src, dst_ref=dst, send_sem=ss, recv_sem=rs, device_id=device, device_id_type=MESH
        )

    def xq(h):
        r = pl.ds(h * ch, ch)
        return remote(q_ref.at[r, pl.ds(theirs, half)], Q.at[z, 1, r], xq_s.at[h], xq_r.at[h], partner)

    def xd(k):
        r = pl.ds(k * dch, dch)
        return remote(d_ref.at[r, pl.ds(theirs, half)], D.at[1, r], xd_s.at[k], xd_r.at[k], partner)

    def chunk(zq, sub):
        return Q.at[zq, sub // 2, pl.ds(pl.multiple_of(sub % 2 * ch, ch), ch)]

    def going_up(i):
        at = chunk(z - i // 4, i % 4)
        return remote(at, at, up_s.at[i], up_r.at[i], above)

    def going_down(i):
        at = chunk(z + i // 4, i % 4)
        return remote(at, at, dn_s.at[i], dn_r.at[i], below)

    def from_below(i):
        at = chunk(z - 1 - i // 4, i % 4)
        return remote(at, at, up_s.at[i], up_r.at[i], above)

    def from_above(i):
        at = chunk(z + 1 + i // 4, i % 4)
        return remote(at, at, dn_s.at[i], dn_r.at[i], below)

    def send_both(i):
        @pl.when(has_above)
        def _():
            going_up(i).start()

        @pl.when(has_below)
        def _():
            going_down(i).start()

    for h in range(2):
        xq(h).start()
    own_q.wait()
    for h in range(2):
        send_both(h)
    for h in range(2):
        xq(h).wait_recv()
        send_both(2 + h)
    for k in range(xd_s.shape[0]):
        xd(k).start()

    n_above, n_below = 4 * (nz - 1 - z), 4 * z

    def relay(j, _):
        @pl.when(j < n_above)
        def _():
            from_above(j).wait_recv()

            @pl.when(has_below)
            def _():
                going_down(j + 4).start()

        @pl.when(j < n_below)
        def _():
            from_below(j).wait_recv()

            @pl.when(has_above)
            def _():
                going_up(j + 4).start()

        return 0

    lax.fori_loop(0, 4 * (nz - 2), relay, 0)
    own_d.wait()
    for k in range(xd_s.shape[0]):
        xd(k).wait_recv()

    def core(t):
        return remote(CS.at[t], CR.at[t], c_s.at[t], c_r.at[t], other)

    def out(t):
        swapped = t + 1 - 2 * (t % 2)
        return remote(ACC.at[t, 1], XR.at[swapped], o_s.at[t], o_r.at[swapped], partner)

    def arrived(t):
        return remote(ACC.at[t, 1], XR.at[t], o_s.at[t], o_r.at[t], partner)

    def z_of(t):
        return jnp.where(z < nz // 2, t // 2, nz - 1 - t // 2)

    def multiply(t):
        queries = Q[z_of(t), t % 2]
        for core_half, into in ((1 - c, CS), (c, ACC)):
            lines = pl.ds(pl.multiple_of(core_half * nd, nd), nd)
            for who in (1, 0):
                into[t, who] = lax.dot_general(
                    D[who, lines, :], queries, NT, preferred_element_type=jnp.float32
                )
            if into is CS:
                core(t).start()

    def hand_over(t):
        core(t).wait_recv()
        ACC[t, 1] = ACC[t, 1] + CR[t, 1]
        out(t).start()
        ACC[t, 0] = ACC[t, 0] + CR[t, 0]

    def step(t, _):
        @pl.when((t >= 2 * nz - 2) & (z == 0))
        def _():
            for h in range(2):
                from_above(2 * t - 4 + h).wait_recv()

        @pl.when((t >= 2 * nz - 2) & (z == nz - 1))
        def _():
            for h in range(2):
                from_below(2 * t - 4 + h).wait_recv()

        multiply(t)

        @pl.when(t > 0)
        def _():
            hand_over(t - 1)

        return 0

    lax.fori_loop(0, 2 * nz, step, 0)
    hand_over(2 * nz - 1)

    def finish(t, _):
        arrived(t).wait_recv()
        origin = jnp.where(t % 2 == 0, x, 1 - x)
        at = pl.multiple_of((z_of(t) * 2 + origin) * rows, rows)
        o_ref[:, pl.ds(at, rows)] = ACC[t, 0] + XR[t]
        return 0

    lax.fori_loop(0, 2 * nz, finish, 0)

    for h in range(2):
        xq(h).wait_send()
    for k in range(xd_s.shape[0]):
        xd(k).wait_send()

    def drain(t, _):
        core(t).wait_send()
        out(t).wait_send()
        return 0

    lax.fori_loop(0, 2 * nz, drain, 0)

    @pl.when(has_above)
    def _():
        lax.fori_loop(0, 4 * (z + 1), lambda i, _: (going_up(i).wait_send(), 0)[1], 0)

    @pl.when(has_below)
    def _():
        lax.fori_loop(0, 4 * (nz - z), lambda i, _: (going_down(i).wait_send(), 0)[1], 0)


def exchange(queries, documents, n):
    rows, k = queries.shape
    nd = documents.shape[0] // 2
    nz, half, dc = n // 2, k // 2, 4
    steps = 2 * nz
    block = (nd, rows)
    dma = pltpu.SemaphoreType.DMA
    return pl.pallas_call(
        functools.partial(kernel, nz),
        out_shape=jax.ShapeDtypeStruct((nd, n * rows), jnp.float32),
        in_specs=[pl.BlockSpec(memory_space=pl.ANY)] * 2,
        out_specs=pl.BlockSpec(memory_space=pltpu.VMEM),
        scratch_shapes=[
            pltpu.VMEM((nz, 2, rows, half), jnp.bfloat16),
            pltpu.VMEM((2, 2 * nd, half), jnp.bfloat16),
            pltpu.VMEM((steps, 2) + block, jnp.float32),
            pltpu.VMEM((steps, 2) + block, jnp.float32),
            pltpu.VMEM((steps, 2) + block, jnp.float32),
            pltpu.VMEM((steps,) + block, jnp.float32),
            dma((2,)),
            dma((2,)), dma((2,)), dma((dc,)), dma((dc,)),
            dma((4 * nz,)), dma((4 * nz,)), dma((4 * nz,)), dma((4 * nz,)),
            dma((steps,)), dma((steps,)), dma((steps,)), dma((steps,)),
        ],
        compiler_params=pltpu.CompilerParams(
            collective_id=0, has_side_effects=True, vmem_limit_bytes=48 * 2**20
        ),
        cost_estimate=pl.CostEstimate(
            flops=4 * n * rows * nd * k, bytes_accessed=32 * 2**20, transcendentals=0
        ),
    )(queries, documents)


def on_device(n, query_grads, doc_grads, query_ids, doc_ids):
    queries = query_grads.reshape(query_grads.shape[0], -1)
    documents = doc_grads.reshape(doc_grads.shape[0], -1)
    rows, nd = queries.shape[0], documents.shape[0] // 2
    if rows % 128 or nd % 16 or n % 2 or n < 4 or n * rows > 1024 or queries.shape[1] % 256:
        every = lax.all_gather(queries, "doc", axis=0, tiled=True)
        raw = lax.dot_general(every, documents, NT, preferred_element_type=jnp.float32)
        same = query_ids[:, None] == doc_ids[None, :]
        partial_scores = jnp.where(same, jnp.zeros_like(raw), raw)
        return lax.psum_scatter(partial_scores, "layer", scatter_dimension=1, tiled=True)
    raw = exchange(queries, documents, n)
    ids = lax.dynamic_slice(doc_ids, (lax.axis_index("layer") * nd,), (nd,))
    return jnp.where(ids[:, None] == query_ids[None, :], jnp.zeros_like(raw), raw).T


def solution(mesh):
    in_specs = (
        P(("grp", "doc"), "layer", None),
        P(("grp", "doc"), "layer", None),
        P("grp"),
        P(("grp", "doc")),
    )
    out_specs = P("grp", ("doc", "layer"))
    return jax.shard_map(
        functools.partial(on_device, mesh.shape["doc"]),
        mesh=mesh, in_specs=in_specs, out_specs=out_specs, check_vma=False,
    )
```

time: 160 us -> 85.9 us (0.54)
  waiting for transfers between devices: 138 us -> 0 us
  Pallas kernels: 0 us -> 80.8 us
  between operations: 13.4 us -> 0.02 us
  matrix products: 8.06 us -> 0 us
  local copies, waits for them, and re-layouts: 0.01 us -> 3.87 us
    all_gather x1 -> x0, waiting for transfers between devices: 130 us -> none  [on_device(): every = lax.all_gather(queries, 'doc', axis=0, tiled=True)]
    pallas_call x0 -> x1, Pallas kernels: none -> 80.8 us  [exchange(): pl.pallas_call(functools.partial(kernel, nz), out_shape=jax.ShapeDtypeStr...]
    dot_general x1 -> x0, matrix products: 8.06 us -> none  [on_device(): lax.dot_general(every, documents, (((1,), (1,)), ((), ())), preferred_ele...]
    reduce_scatter x1 -> x0, waiting for transfers between devices: 7.4 us -> none  [on_device(): lax.psum_scatter(partial_scores, 'layer', scatter_dimension=1, tiled=True)]
    unnamed x2 -> x6, local copies, waits for them, and re-layouts: 0.01 us -> 3.12 us
  transfers between devices with their start and end apart: 2 -> 0, of which waited for: 2 -> 0; matrix products, arithmetic and copies ran while one was open for 0% -> 0% of each run, Pallas kernels for 0% -> 0%
where the time goes in v1:
time: 85.9 us; the launch traced here: 85.7 us
  Pallas kernels  80.8 us (94%)
  local copies, waits for them, and re-layouts  3.87 us (5%)
  other arithmetic  1 us (1%)
    pallas_call x1, Pallas kernels, exchange(): pl.pallas_call(functools.partial(kernel, nz), out_shape=jax.ShapeDtypeStr...  80.8 us
    unnamed x6, local copies, waits for them, and re-layouts  3.12 us

profile of v1, /device:TPU:0, one launch (start us, length us, event | category | flops | bytes accessed | tf_op | source)
XLA Modules:
  0.0 85.7 jit_solution(17583269738096198346)
XLA Ops:
  0.0 0.8 dynamic_slice.3
  0.8 0.0 copy-start
  0.8 1.9 %copy-done = bf16[384,1,4096]{2,0,1:T(8,128)(2,1)S(1)} copy-done((bf16[384,1,4096]{2,0,1:T(8,128)(2,1)S(1)}, bf16[384,1,4096]{2,0,1:T(8,128)(2,1)}, u32[]{:S(2)}) %copy-start) | copy-done | bytes 3145752
  2.6 0.0 copy-start.1
  2.6 1.2 %copy-done.1 = bf16[128,1,4096]{2,0,1:T(8,128)(2,1)S(1)} copy-done((bf16[128,1,4096]{2,0,1:T(8,128)(2,1)S(1)}, bf16[128,1,4096]{2,0,1:T(8,128)(2,1)}, u32[]{:S(2)}) %copy-start.1) | copy-done | bytes 1048600
  3.9 0.0 copy-start.2
  3.9 80.8 %shard_map.46 = f32[192,1024]{1,0:T(8,128)S(1)} custom-call(bf16[128,4096]{1,0:T(8,128)(2,1)S(1)} %bitcast.5, bf16[384,4096]{1,0:T(8,128)(2,1)S(1)} %bitcast.4), custom_call_target="tpu_custom_call" | custom-call | flops 3221225472 | bytes 33554432 | tf_op jit(solution)/shard_map/pallas_call | solution.py:219
  84.7 0.0 copy-done.2
  84.7 1.0 %select_bitcast_fusion = f32[1024,192]{0,1:T(8,128)} fusion(f32[192,1024]{1,0:T(8,128)S(1)} %shard_map.46, s32[1024]{0:T(1024)S(1)} %copy-done.2, s32[192]{0:T(256)S(1)} %dynamic_slice.3), kind=kLoop, calls=%fused_computation | loop fusion | flops 393216 | bytes 1577728 | tf_op jit(solution)/shard_map/transpose | solution.py:257
Async XLA Ops:
  0.8 1.9 %copy-start = (bf16[384,1,4096]{2,0,1:T(8,128)(2,1)S(1)}, bf16[384,1,4096]{2,0,1:T(8,128)(2,1)}, u32[]{:S(2)}) copy-start(bf16[384,1,4096]{2,0,1:T(8,128)(2,1)} %param.5) | copy-start | bytes 9437188
  2.6 1.2 %copy-start.1 = (bf16[128,1,4096]{2,0,1:T(8,128)(2,1)S(1)}, bf16[128,1,4096]{2,0,1:T(8,128)(2,1)}, u32[]{:S(2)}) copy-start(bf16[128,1,4096]{2,0,1:T(8,128)(2,1)} %param.4) | copy-start | bytes 3145732
  3.9 80.9 %copy-start.2 = (s32[1024]{0:T(1024)S(1)}, s32[1024]{0:T(1024)}, u32[]{:S(2)}) copy-start(s32[1024]{0:T(1024)} %param.6) | copy-start | bytes 12292

commit v2 on v1

v2 whole, which is shorter than its diff:
```python
import functools
import math

import jax
import jax.numpy as jnp
from jax import lax
from jax.experimental import pallas as pl
from jax.experimental.pallas import tpu as pltpu
from jax.sharding import PartitionSpec as P

MESH = pl.DeviceIdType.MESH
NT = (((1,), (1,)), ((), ()))
STEP = math.log(2) / 128
TOP = 32700.0


def encode(into, sums):
    n = sums.shape[0]
    peak = jnp.maximum(jnp.max(jnp.abs(sums), axis=0, keepdims=True), 1e-30)
    level = jnp.ceil(jnp.log(peak) / STEP) + 1
    units = jnp.round(sums * (jnp.exp(level * -STEP) * TOP))
    into[pl.ds(0, n)] = units.astype(jnp.int32).astype(jnp.int16)
    level = jnp.broadcast_to(level.astype(jnp.int32), (16, sums.shape[1]))
    into[pl.ds(n, 16)] = level.astype(jnp.int16)


def decode(coded):
    n = coded.shape[0] - 16
    level = coded[pl.ds(n, 16)].astype(jnp.int32).astype(jnp.float32)[:1]
    units = coded[pl.ds(0, n)].astype(jnp.int32).astype(jnp.float32)
    return units * (jnp.exp(level * STEP) / TOP)


def kernel(
    nz, q_ref, d_ref, o_ref, QA, QB, DA, DB, HA, CS, CR, ACC, XS, XR, HCS, HCR, HACC, HS, RET,
    loc, xq_s, xq_r, xd_s, xd_r, up_s, up_r, dn_s, dn_r, h_s, h_r, c_s, c_r, o_s, o_r, hc_s, hc_r, ret_s, ret_r,
):
    g, d, c = lax.axis_index("grp"), lax.axis_index("doc"), lax.axis_index("layer")
    z, x = d // 2, d % 2
    partner, other = (g, d + 1 - 2 * x, c), (g, d, 1 - c)
    above, below = (g, d + 2, c), (g, d - 2, c)
    has_above, has_below = z < nz - 1, z > 0
    is_end = (z == 0) | (z == nz - 1)
    is_helper = (z == 1) | (z == nz - 2)
    helper = (g, jnp.where(z == 0, d + 2, d - 2), c)
    helped = (g, jnp.where(z == 1, d - 2, d + 2), c)
    rows, ka, kb = QA.shape[2], QA.shape[3], QB.shape[3]
    half = ka + kb
    ch = rows // 2
    nd = DA.shape[1] // 2

    def columns(part, mine):
        start = jnp.where(mine, x, 1 - x) * half + (ka if part else 0)
        return pl.ds(pl.multiple_of(start, 128), kb if part else ka)

    barrier = pltpu.get_barrier_semaphore()

    def greet(device):
        pl.semaphore_signal(barrier, inc=1, device_id=device, device_id_type=MESH)

    greet(partner)
    greet(other)

    @pl.when(has_above)
    def _():
        greet(above)

    @pl.when(has_below)
    def _():
        greet(below)

    def own(part):
        Q, D = (QA, QB)[part], (DA, DB)[part]
        return (
            pltpu.make_async_copy(q_ref.at[:, columns(part, True)], Q.at[z, 0], loc.at[part]),
            pltpu.make_async_copy(d_ref.at[:, columns(part, True)], D.at[0], loc.at[2 + part]),
        )

    for kind in (0, 1):
        for part in (0, 1):
            own(part)[kind].start()
    pl.semaphore_wait(barrier, 2 + jnp.where(has_above, 1, 0) + jnp.where(has_below, 1, 0))

    def remote(src, dst, ss, rs, device):
        return pltpu.make_async_remote_copy(
            src_ref=src, dst_ref=dst, send_sem=ss, recv_sem=rs, device_id=device, device_id_type=MESH
        )

    def xq(h, part):
        r = pl.ds(h * ch, ch)
        return remote(
            q_ref.at[r, columns(part, False)], (QA, QB)[part].at[z, 1, r], xq_s.at[h, part], xq_r.at[h, part], partner
        )

    def xd(h, part):
        r = pl.ds(h * nd, nd)
        return remote(
            d_ref.at[r, columns(part, False)], (DA, DB)[part].at[1, r], xd_s.at[h, part], xd_r.at[h, part], partner
        )

    def chunk(part, zq, sub):
        return (QA, QB)[part].at[zq, sub // 2, pl.ds(pl.multiple_of(sub % 2 * ch, ch), ch)]

    def going_up(i, part):
        at = chunk(part, z - i // 4, i % 4)
        return remote(at, at, up_s.at[i, part], up_r.at[i, part], above)

    def going_down(i, part):
        at = chunk(part, z + i // 4, i % 4)
        return remote(at, at, dn_s.at[i, part], dn_r.at[i, part], below)

    def from_below(i, part):
        at = chunk(part, z - 1 - i // 4, i % 4)
        return remote(at, at, up_s.at[i, part], up_r.at[i, part], above)

    def from_above(i, part):
        at = chunk(part, z + 1 + i // 4, i % 4)
        return remote(at, at, dn_s.at[i, part], dn_r.at[i, part], below)

    def both_parts(act, with_b, with_a):
        @pl.when(with_b)
        def _():
            act(1)

        @pl.when(with_a)
        def _():
            act(0)

    def send_up(i):
        both_parts(lambda part: going_up(i, part).start(), has_above, z < nz - 2)

    def send_down(i):
        both_parts(lambda part: going_down(i, part).start(), has_below, z > 1)

    for h in range(2):
        for part in (1, 0):
            xq(h, part).start()
    for part in (0, 1):
        own(part)[0].wait()
    for h in range(2):
        send_up(h)
        send_down(h)
    for h in range(2):
        for part in (1, 0):
            xq(h, part).wait_recv()
        send_up(2 + h)
        send_down(2 + h)
    for part in (0, 1):
        for h in range(2):
            xd(h, part).start()
    for part in (0, 1):
        own(part)[1].wait()

    def lend(who, h):
        at = pl.ds(h * nd, nd)
        return remote(DA.at[who, at], HA.at[who, at], h_s.at[who, h], h_r.at[who, h], helper)

    @pl.when(is_end)
    def _():
        for h in range(2):
            lend(0, h).start()
        for h in range(2):
            xd(h, 0).wait_recv()
            lend(1, h).start()

    n_above, n_below = 4 * (nz - 1 - z), 4 * z

    def relay(j, _):
        @pl.when(j < n_above)
        def _():
            both_parts(lambda part: from_above(j, part).wait_recv(), True, has_below)
            send_down(j + 4)

        @pl.when(j < n_below)
        def _():
            both_parts(lambda part: from_below(j, part).wait_recv(), True, has_above)
            send_up(j + 4)

        return 0

    lax.fori_loop(0, 4 * (nz - 2), relay, 0)

    @pl.when(~is_end)
    def _():
        for h in range(2):
            xd(h, 0).wait_recv()

    for h in range(2):
        xd(h, 1).wait_recv()

    def core(t):
        return remote(CS.at[t], CR.at[t], c_s.at[t], c_r.at[t], other)

    def helper_core(t):
        return remote(HCS.at[t], HCR.at[t], hc_s.at[t], hc_r.at[t], other)

    def give_back(t):
        return remote(HS.at[t], RET.at[t], ret_s.at[t], ret_r.at[t], helped)

    def out(t):
        swapped = t + 1 - 2 * (t % 2)
        return remote(XS.at[t], XR.at[swapped], o_s.at[t], o_r.at[swapped], partner)

    def arrived(t):
        return remote(XS.at[t], XR.at[t], o_s.at[t], o_r.at[t], partner)

    def z_of(o):
        return jnp.where(z < nz // 2, o, nz - 1 - o)

    def product(documents, queries):
        return lax.dot_general(documents, queries, NT, preferred_element_type=jnp.float32)

    def pair(ref, zq):
        return ref[zq].reshape(2 * rows, ref.shape[3])

    def lines(core_half):
        return pl.ds(pl.multiple_of(core_half * nd, nd), nd)

    def multiply(o):
        zq = z_of(o)
        for core_half, into in ((1 - c, CS), (c, ACC)):
            for who in (1, 0):
                part = product(DB[who, lines(core_half), :], pair(QB, zq))
                for s in (0, 1):
                    into[2 * o + s, who] = part[:, s * rows : (s + 1) * rows]

                @pl.when((~is_end) | (o == 0))
                def _():
                    more = product(DA[who, lines(core_half), :], pair(QA, zq))
                    for s in (0, 1):
                        into[2 * o + s, who] = into[2 * o + s, who] + more[:, s * rows : (s + 1) * rows]

            if into is CS:
                for s in (0, 1):
                    core(2 * o + s).start()

    def help_multiply(o):
        zq = jnp.where(z == 1, 1 + o, nz - 2 - o)
        for core_half, into in ((1 - c, HCS), (c, HACC)):
            for who in (1, 0):
                part = product(HA[who, lines(core_half), :], pair(QA, zq))
                for s in (0, 1):
                    into[2 * o + s, who] = part[:, s * rows : (s + 1) * rows]
            if into is HCS:
                for s in (0, 1):
                    helper_core(2 * o + s).start()

    def help_hand_over(o):
        for s in (0, 1):
            t = 2 * o + s
            helper_core(t).wait_recv()
            for who in (1, 0):
                encode(HS.at[t, who], HACC[t, who] + HCR[t, who])
            give_back(t).start()

    def hand_over(o):
        @pl.when(is_end & (o > 0))
        def _():
            for s in (0, 1):
                t = 2 * o + s
                give_back(t - 2).wait_recv()
                for who in (1, 0):
                    ACC[t, who] = ACC[t, who] + decode(RET.at[t - 2, who])

        for s in (0, 1):
            t = 2 * o + s
            core(t).wait_recv()
            encode(XS.at[t], ACC[t, 1] + CR[t, 1])
            out(t).start()
            ACC[t, 0] = ACC[t, 0] + CR[t, 0]

    @pl.when(is_helper)
    def _():
        for who in (0, 1):
            for h in range(2):
                lend(who, h).wait_recv()

    def step(o, _):
        @pl.when((o == nz - 1) & (z == 0))
        def _():
            for h in range(4):
                from_above(4 * (nz - 2) + h, 1).wait_recv()

        @pl.when((o == nz - 1) & (z == nz - 1))
        def _():
            for h in range(4):
                from_below(4 * (nz - 2) + h, 1).wait_recv()

        @pl.when(is_helper & (o < nz - 1))
        def _():
            help_multiply(o)

        multiply(o)

        @pl.when(is_helper & (o < nz - 1))
        def _():
            help_hand_over(o)

        @pl.when(o > 0)
        def _():
            hand_over(o - 1)

        return 0

    lax.fori_loop(0, nz, step, 0)
    hand_over(nz - 1)

    def finish(t, _):
        arrived(t).wait_recv()
        origin = jnp.where(t % 2 == 0, x, 1 - x)
        at = pl.multiple_of((z_of(t // 2) * 2 + origin) * rows, rows)
        o_ref[:, pl.ds(at, rows)] = ACC[t, 0] + decode(XR.at[t])
        return 0

    lax.fori_loop(0, 2 * nz, finish, 0)

    for h in range(2):
        for part in (0, 1):
            xq(h, part).wait_send()
            xd(h, part).wait_send()

    def drain(t, _):
        core(t).wait_send()
        out(t).wait_send()
        return 0

    lax.fori_loop(0, 2 * nz, drain, 0)

    @pl.when(is_end)
    def _():
        for who in (0, 1):
            for h in range(2):
                lend(who, h).wait_send()

    @pl.when(is_helper)
    def _():
        def drain_help(t, _):
            helper_core(t).wait_send()
            give_back(t).wait_send()
            return 0

        lax.fori_loop(0, 2 * nz - 2, drain_help, 0)

    def drain_up(i, _):
        both_parts(lambda part: going_up(i, part).wait_send(), True, z < nz - 2)
        return 0

    def drain_down(i, _):
        both_parts(lambda part: going_down(i, part).wait_send(), True, z > 1)
        return 0

    @pl.when(has_above)
    def _():
        lax.fori_loop(0, 4 * (z + 1), drain_up, 0)

    @pl.when(has_below)
    def _():
        lax.fori_loop(0, 4 * (nz - z), drain_down, 0)


def exchange(queries, documents, n):
    rows, k = queries.shape
    nd = documents.shape[0] // 2
    nz, half = n // 2, k // 2
    ka = half // 128 * 3 // 8 * 128
    kb = half - ka
    steps, helps = 2 * nz, 2 * nz - 2
    block, coded = (nd, rows), (nd + 16, rows)
    dma = pltpu.SemaphoreType.DMA
    return pl.pallas_call(
        functools.partial(kernel, nz),
        out_shape=jax.ShapeDtypeStruct((nd, n * rows), jnp.float32),
        in_specs=[pl.BlockSpec(memory_space=pl.ANY)] * 2,
        out_specs=pl.BlockSpec(memory_space=pltpu.VMEM),
        scratch_shapes=[
            pltpu.VMEM((nz, 2, rows, ka), jnp.bfloat16),
            pltpu.VMEM((nz, 2, rows, kb), jnp.bfloat16),
            pltpu.VMEM((2, 2 * nd, ka), jnp.bfloat16),
            pltpu.VMEM((2, 2 * nd, kb), jnp.bfloat16),
            pltpu.VMEM((2, 2 * nd, ka), jnp.bfloat16),
            pltpu.VMEM((steps, 2) + block, jnp.float32),
            pltpu.VMEM((steps, 2) + block, jnp.float32),
            pltpu.VMEM((steps, 2) + block, jnp.float32),
            pltpu.VMEM((steps,) + coded, jnp.int16),
            pltpu.VMEM((steps,) + coded, jnp.int16),
            pltpu.VMEM((helps, 2) + block, jnp.float32),
            pltpu.VMEM((helps, 2) + block, jnp.float32),
            pltpu.VMEM((helps, 2) + block, jnp.float32),
            pltpu.VMEM((helps, 2) + coded, jnp.int16),
            pltpu.VMEM((helps, 2) + coded, jnp.int16),
            dma((4,)),
            dma((2, 2)), dma((2, 2)), dma((2, 2)), dma((2, 2)),
            dma((4 * nz, 2)), dma((4 * nz, 2)), dma((4 * nz, 2)), dma((4 * nz, 2)),
            dma((2, 2)), dma((2, 2)),
            dma((steps,)), dma((steps,)), dma((steps,)), dma((steps,)),
            dma((helps,)), dma((helps,)), dma((helps,)), dma((helps,)),
        ],
        compiler_params=pltpu.CompilerParams(
            collective_id=0, has_side_effects=True, vmem_limit_bytes=60 * 2**20
        ),
        cost_estimate=pl.CostEstimate(
            flops=4 * n * rows * nd * k, bytes_accessed=32 * 2**20, transcendentals=0
        ),
    )(queries, documents)


def on_device(n, query_grads, doc_grads, query_ids, doc_ids):
    queries = query_grads.reshape(query_grads.shape[0], -1)
    documents = doc_grads.reshape(doc_grads.shape[0], -1)
    rows, nd = queries.shape[0], documents.shape[0] // 2
    if rows % 128 or nd % 16 or n % 2 or n < 8 or n * rows > 1024 or queries.shape[1] % 2048:
        every = lax.all_gather(queries, "doc", axis=0, tiled=True)
        raw = lax.dot_general(every, documents, NT, preferred_element_type=jnp.float32)
        same = query_ids[:, None] == doc_ids[None, :]
        partial_scores = jnp.where(same, jnp.zeros_like(raw), raw)
        return lax.psum_scatter(partial_scores, "layer", scatter_dimension=1, tiled=True)
    raw = exchange(queries, documents, n)
    ids = jnp.where(lax.axis_index("layer") == 0, doc_ids[:nd], doc_ids[nd:])
    return jnp.where(ids[:, None] == query_ids[None, :], jnp.zeros_like(raw), raw).T


def solution(mesh):
    in_specs = (
        P(("grp", "doc"), "layer", None),
        P(("grp", "doc"), "layer", None),
        P("grp"),
        P(("grp", "doc")),
    )
    out_specs = P("grp", ("doc", "layer"))
    return jax.shard_map(
        functools.partial(on_device, mesh.shape["doc"]),
        mesh=mesh, in_specs=in_specs, out_specs=out_specs, check_vma=False,
    )
```

time: 85.9 us -> 80.7 us (0.939)
  local copies, waits for them, and re-layouts: 3.87 us -> 0.01 us
  Pallas kernels: 80.8 us -> 77.5 us
  other arithmetic: 1 us -> 2.96 us
    pallas_call x1, Pallas kernels: 80.8 us -> 77.5 us  [exchange(): pl.pallas_call(functools.partial(kernel, nz), out_shape=jax.ShapeDtypeStr...]
    unnamed x6 -> x2, local copies, waits for them, and re-layouts: 3.12 us -> 0.01 us
    transpose x1, other arithmetic: 1 us -> 2.13 us  [on_device(): jnp.where(ids[:, None] == query_ids[None, :], jnp.zeros_like(raw), raw)]
where the time goes in v2:
time: 80.7 us; the launch traced here: 80.5 us
  Pallas kernels  77.5 us (96%)
  other arithmetic  2.96 us (4%)
    pallas_call x1, Pallas kernels, exchange(): pl.pallas_call(functools.partial(kernel, nz), out_shape=jax.ShapeDtypeStr...  77.5 us
    transpose x1, other arithmetic, on_device(): jnp.where(ids[:, None] == query_ids[None, :], jnp.zeros_like(raw), raw)  2.13 us

profile of v2, /device:TPU:0, one launch (start us, length us, event | category | flops | bytes accessed | tf_op | source)
XLA Modules:
  0.0 80.5 jit_solution(18137049923394834775)
XLA Ops:
  0.0 0.8 %slice_select_fusion = s32[192]{0:T(256)S(1)} fusion(s32[384]{0:T(512)} %param.7, pred[]{:T(512)S(6)} %eq.16), kind=kLoop, calls=%fused_computation.1 | loop fusion | flops 192 | bytes 2305 | tf_op jit(solution)/shard_map/jit(_where)/select_n | solution.py:418
  0.8 0.0 copy-start
  0.8 77.5 %shard_map.46 = f32[192,1024]{1,0:T(8,128)} custom-call(bf16[128,4096]{1,0:T(8,128)(2,1)} %bitcast.5, bf16[384,4096]{1,0:T(8,128)(2,1)} %bitcast.4), custom_call_target="tpu_custom_call" | custom-call | flops 3221225472 | bytes 33554432 | tf_op jit(solution)/shard_map/pallas_call | solution.py:370
  78.4 0.0 copy-done
  78.4 2.1 %select_bitcast_fusion = f32[1024,192]{0,1:T(8,128)} fusion(f32[192,1024]{1,0:T(8,128)} %shard_map.46, s32[1024]{0:T(1024)S(1)} %copy-done, s32[192]{0:T(256)S(1)} %slice_select_fusion), kind=kLoop, calls=%fused_computation | loop fusion | flops 393216 | bytes 1577728 | tf_op jit(solution)/shard_map/transpose | solution.py:419
Async XLA Ops:
  0.8 77.6 %copy-start = (s32[1024]{0:T(1024)S(1)}, s32[1024]{0:T(1024)}, u32[]{:S(2)}) copy-start(s32[1024]{0:T(1024)} %param.6) | copy-start | bytes 12292

commit v3 on v2

--- a/solution.py
+++ b/solution.py
@@ -32,7 +32,7 @@
 
 
 def kernel(
-    nz, q_ref, d_ref, o_ref, QA, QB, DA, DB, HA, CS, CR, ACC, XS, XR, HCS, HCR, HACC, HS, RET,
+    nz, q_ref, d_ref, o_ref, QA, QB, DA, DB, HA, SUM, CR, XS, XR, HSUM, HCR, HS, RET,
     loc, xq_s, xq_r, xd_s, xd_r, up_s, up_r, dn_s, dn_r, h_s, h_r, c_s, c_r, o_s, o_r, hc_s, hc_r, ret_s, ret_r,
 ):
     g, d, c = lax.axis_index("grp"), lax.axis_index("doc"), lax.axis_index("layer")
@@ -76,9 +76,9 @@
             pltpu.make_async_copy(d_ref.at[:, columns(part, True)], D.at[0], loc.at[2 + part]),
         )
 
-    for kind in (0, 1):
-        for part in (0, 1):
-            own(part)[kind].start()
+    for part in (0, 1):
+        for copy in own(part):
+            copy.start()
     pl.semaphore_wait(barrier, 2 + jnp.where(has_above, 1, 0) + jnp.where(has_below, 1, 0))
 
     def remote(src, dst, ss, rs, device):
@@ -158,10 +158,10 @@
     @pl.when(is_end)
     def _():
         for h in range(2):
-            lend(0, h).start()
-        for h in range(2):
             xd(h, 0).wait_recv()
             lend(1, h).start()
+        for h in range(2):
+            lend(0, h).start()
 
     n_above, n_below = 4 * (nz - 1 - z), 4 * z
 
@@ -178,31 +178,17 @@
 
         return 0
 
-    lax.fori_loop(0, 4 * (nz - 2), relay, 0)
-
-    @pl.when(~is_end)
-    def _():
-        for h in range(2):
-            xd(h, 0).wait_recv()
-
-    for h in range(2):
-        xd(h, 1).wait_recv()
-
-    def core(t):
-        return remote(CS.at[t], CR.at[t], c_s.at[t], c_r.at[t], other)
-
-    def helper_core(t):
-        return remote(HCS.at[t], HCR.at[t], hc_s.at[t], hc_r.at[t], other)
-
-    def give_back(t):
-        return remote(HS.at[t], RET.at[t], ret_s.at[t], ret_r.at[t], helped)
-
-    def out(t):
-        swapped = t + 1 - 2 * (t % 2)
-        return remote(XS.at[t], XR.at[swapped], o_s.at[t], o_r.at[swapped], partner)
-
-    def arrived(t):
-        return remote(XS.at[t], XR.at[t], o_s.at[t], o_r.at[t], partner)
+    def core(o, who):
+        return remote(SUM.at[1, o, who], CR.at[o, who], c_s.at[o, who], c_r.at[o, who], other)
+
+    def helper_core(o, who):
+        return remote(HSUM.at[1, o, who], HCR.at[o, who], hc_s.at[o, who], hc_r.at[o, who], other)
+
+    def give_back(o, who):
+        return remote(HS.at[o, who], RET.at[o, who], ret_s.at[o, who], ret_r.at[o, who], helped)
+
+    def out(o):
+        return remote(XS.at[o], XR.at[o], o_s.at[o], o_r.at[o], partner)
 
     def z_of(o):
         return jnp.where(z < nz // 2, o, nz - 1 - o)
@@ -213,118 +199,155 @@
     def pair(ref, zq):
         return ref[zq].reshape(2 * rows, ref.shape[3])
 
-    def lines(core_half):
-        return pl.ds(pl.multiple_of(core_half * nd, nd), nd)
-
-    def multiply(o):
-        zq = z_of(o)
-        for core_half, into in ((1 - c, CS), (c, ACC)):
-            for who in (1, 0):
-                part = product(DB[who, lines(core_half), :], pair(QB, zq))
-                for s in (0, 1):
-                    into[2 * o + s, who] = part[:, s * rows : (s + 1) * rows]
-
-                @pl.when((~is_end) | (o == 0))
-                def _():
-                    more = product(DA[who, lines(core_half), :], pair(QA, zq))
-                    for s in (0, 1):
-                        into[2 * o + s, who] = into[2 * o + s, who] + more[:, s * rows : (s + 1) * rows]
-
-            if into is CS:
-                for s in (0, 1):
-                    core(2 * o + s).start()
-
-    def help_multiply(o):
-        zq = jnp.where(z == 1, 1 + o, nz - 2 - o)
-        for core_half, into in ((1 - c, HCS), (c, HACC)):
-            for who in (1, 0):
-                part = product(HA[who, lines(core_half), :], pair(QA, zq))
-                for s in (0, 1):
-                    into[2 * o + s, who] = part[:, s * rows : (s + 1) * rows]
-            if into is HCS:
-                for s in (0, 1):
-                    helper_core(2 * o + s).start()
-
-    def help_hand_over(o):
+    def each(low, high, body):
+        lax.fori_loop(low, high, lambda o, _: (body(o), 0)[1], 0)
+
+    def multiply(who, h, low, high):
+        lines, slot = pl.ds(h * nd, nd), jnp.where(c == h, 0, 1)
+
+        def body(o):
+            zq = z_of(o)
+            SUM[slot, o, who] = product(DB[who, lines, :], pair(QB, zq))
+
+            @pl.when((~is_end) | (o == 0))
+            def _():
+                SUM[slot, o, who] = SUM[slot, o, who] + product(DA[who, lines, :], pair(QA, zq))
+
+            @pl.when(c != h)
+            def _():
+                core(o, who).start()
+
+        each(low, high, body)
+
+    def add_up(who, h, low, high):
+        def body(o):
+            core(o, who).wait_recv()
+            SUM[0, o, who] = SUM[0, o, who] + CR[o, who]
+
+            @pl.when(is_end & (o > 0))
+            def _():
+                give_back(o - 1, who).wait_recv()
+                SUM[0, o, who] = SUM[0, o, who] + decode(RET.at[o - 1, who])
+
+            if who == 1:
+                encode(XS.at[o], SUM[0, o, 1])
+                out(o).start()
+
+        @pl.when(c == h)
+        def _():
+            each(low, high, body)
+
+    def help_multiply(who, h, low, high):
+        lines, slot = pl.ds(h * nd, nd), jnp.where(c == h, 0, 1)
+
+        def body(o):
+            zq = jnp.where(z == 1, 1 + o, nz - 2 - o)
+            HSUM[slot, o, who] = product(HA[who, lines, :], pair(QA, zq))
+
+            @pl.when(c != h)
+            def _():
+                helper_core(o, who).start()
+
+        each(low, high, body)
+
+    def help_add_up(who, h, low, high):
+        def body(o):
+            helper_core(o, who).wait_recv()
+            encode(HS.at[o, who], HSUM[0, o, who] + HCR[o, who])
+            give_back(o, who).start()
+
+        @pl.when(c == h)
+        def _():
+            each(low, high, body)
+
+    total = 4 * (nz - 2)
+    first = jnp.where(is_end, total, total - 2)
+    lax.fori_loop(0, first, relay, 0)
+
+    @pl.when(is_helper)
+    def _():
+        for h in range(2):
+            lend(1, h).wait_recv()
+            help_multiply(1, h, 0, nz - 2)
+        for h in range(2):
+            help_add_up(1, h, 0, nz - 2)
+
+    @pl.when(~is_end)
+    def _():
+        for h in range(2):
+            xd(h, 0).wait_recv()
+
+    xd(0, 1).wait_recv()
+    multiply(1, 0, 0, nz - 1)
+    add_up(1, 0, 0, nz - 1)
+    for h in range(2):
+        multiply(0, h, 0, nz - 1)
+
+    lax.fori_loop(first, total, relay, 0)
+
+    @pl.when(is_helper)
+    def _():
+        for h in range(2):
+            help_multiply(1, h, nz - 2, nz - 1)
+        for h in range(2):
+            help_add_up(1, h, nz - 2, nz - 1)
+        lend(0, 0).wait_recv()
+        help_multiply(0, 0, 0, nz - 1)
+
+    @pl.when(z == 0)
+    def _():
+        for h in range(4):
+            from_above(total + h, 1).wait_recv()
+
+    @pl.when(z == nz - 1)
+    def _():
+        for h in range(4):
+            from_below(total + h, 1).wait_recv()
+
+    multiply(1, 0, nz - 1, nz)
+    xd(1, 1).wait_recv()
+    multiply(1, 1, 0, nz)
+
+    @pl.when(is_helper)
+    def _():
+        help_add_up(0, 0, 0, nz - 1)
+        lend(0, 1).wait_recv()
+        help_multiply(0, 1, 0, nz - 1)
+
+    add_up(1, 0, nz - 1, nz)
+    add_up(1, 1, 0, nz)
+
+    @pl.when(is_helper)
+    def _():
+        help_add_up(0, 1, 0, nz - 1)
+
+    for h in range(2):
+        multiply(0, h, nz - 1, nz)
+    for h in range(2):
+        add_up(0, h, 0, nz)
+
+    def finish(o):
+        out(o).wait_recv()
+        sums = decode(XR.at[o])
         for s in (0, 1):
-            t = 2 * o + s
-            helper_core(t).wait_recv()
-            for who in (1, 0):
-                encode(HS.at[t, who], HACC[t, who] + HCR[t, who])
-            give_back(t).start()
-
-    def hand_over(o):
-        @pl.when(is_end & (o > 0))
-        def _():
-            for s in (0, 1):
-                t = 2 * o + s
-                give_back(t - 2).wait_recv()
-                for who in (1, 0):
-                    ACC[t, who] = ACC[t, who] + decode(RET.at[t - 2, who])
-
-        for s in (0, 1):
-            t = 2 * o + s
-            core(t).wait_recv()
-            encode(XS.at[t], ACC[t, 1] + CR[t, 1])
-            out(t).start()
-            ACC[t, 0] = ACC[t, 0] + CR[t, 0]
-
-    @pl.when(is_helper)
-    def _():
-        for who in (0, 1):
-            for h in range(2):
-                lend(who, h).wait_recv()
-
-    def step(o, _):
-        @pl.when((o == nz - 1) & (z == 0))
-        def _():
-            for h in range(4):
-                from_above(4 * (nz - 2) + h, 1).wait_recv()
-
-        @pl.when((o == nz - 1) & (z == nz - 1))
-        def _():
-            for h in range(4):
-                from_below(4 * (nz - 2) + h, 1).wait_recv()
-
-        @pl.when(is_helper & (o < nz - 1))
-        def _():
-            help_multiply(o)
-
-        multiply(o)
-
-        @pl.when(is_helper & (o < nz - 1))
-        def _():
-            help_hand_over(o)
-
-        @pl.when(o > 0)
-        def _():
-            hand_over(o - 1)
-
-        return 0
-
-    lax.fori_loop(0, nz, step, 0)
-    hand_over(nz - 1)
-
-    def finish(t, _):
-        arrived(t).wait_recv()
-        origin = jnp.where(t % 2 == 0, x, 1 - x)
-        at = pl.multiple_of((z_of(t // 2) * 2 + origin) * rows, rows)
-        o_ref[:, pl.ds(at, rows)] = ACC[t, 0] + decode(XR.at[t])
-        return 0
-
-    lax.fori_loop(0, 2 * nz, finish, 0)
+            at = pl.multiple_of((z_of(o) * 2 + jnp.where(x == s, 0, 1)) * rows, rows)
+            mine, theirs = pl.ds(s * rows, rows), slice((1 - s) * rows, (2 - s) * rows)
+            o_ref[:, pl.ds(at, rows)] = SUM[0, o, 0, :, mine] + sums[:, theirs]
+
+    each(0, nz, finish)
 
     for h in range(2):
         for part in (0, 1):
             xq(h, part).wait_send()
             xd(h, part).wait_send()
 
-    def drain(t, _):
-        core(t).wait_send()
-        out(t).wait_send()
-        return 0
-
-    lax.fori_loop(0, 2 * nz, drain, 0)
+    for h in range(2):
+
+        @pl.when(c != h)
+        def _():
+            each(0, nz, lambda o: [core(o, who).wait_send() for who in (0, 1)])
+
+    each(0, nz, lambda o: out(o).wait_send())
 
     @pl.when(is_end)
     def _():
@@ -334,12 +357,12 @@
 
     @pl.when(is_helper)
     def _():
-        def drain_help(t, _):
-            helper_core(t).wait_send()
-            give_back(t).wait_send()
-            return 0
-
-        lax.fori_loop(0, 2 * nz - 2, drain_help, 0)
+        def drain_help(o):
+            for who in (0, 1):
+                helper_core(o, who).wait_send()
+                give_back(o, who).wait_send()
+
+        each(0, nz - 1, drain_help)
 
     def drain_up(i, _):
         both_parts(lambda part: going_up(i, part).wait_send(), True, z < nz - 2)
@@ -364,13 +387,12 @@
     nz, half = n // 2, k // 2
     ka = half // 128 * 3 // 8 * 128
     kb = half - ka
-    steps, helps = 2 * nz, 2 * nz - 2
-    block, coded = (nd, rows), (nd + 16, rows)
+    block, coded = (nd, 2 * rows), (nd + 16, 2 * rows)
     dma = pltpu.SemaphoreType.DMA
     return pl.pallas_call(
         functools.partial(kernel, nz),
         out_shape=jax.ShapeDtypeStruct((nd, n * rows), jnp.float32),
-        in_specs=[pl.BlockSpec(memory_space=pl.ANY)] * 2,
+        in_specs=[pl.BlockSpec(memory_space=pltpu.HBM)] * 2,
         out_specs=pl.BlockSpec(memory_space=pltpu.VMEM),
         scratch_shapes=[
             pltpu.VMEM((nz, 2, rows, ka), jnp.bfloat16),
@@ -378,25 +400,23 @@
             pltpu.VMEM((2, 2 * nd, ka), jnp.bfloat16),
             pltpu.VMEM((2, 2 * nd, kb), jnp.bfloat16),
             pltpu.VMEM((2, 2 * nd, ka), jnp.bfloat16),
-            pltpu.VMEM((steps, 2) + block, jnp.float32),
-            pltpu.VMEM((steps, 2) + block, jnp.float32),
-            pltpu.VMEM((steps, 2) + block, jnp.float32),
-            pltpu.VMEM((steps,) + coded, jnp.int16),
-            pltpu.VMEM((steps,) + coded, jnp.int16),
-            pltpu.VMEM((helps, 2) + block, jnp.float32),
-            pltpu.VMEM((helps, 2) + block, jnp.float32),
-            pltpu.VMEM((helps, 2) + block, jnp.float32),
-            pltpu.VMEM((helps, 2) + coded, jnp.int16),
-            pltpu.VMEM((helps, 2) + coded, jnp.int16),
+            pltpu.VMEM((2, nz, 2) + block, jnp.float32),
+            pltpu.VMEM((nz, 2) + block, jnp.float32),
+            pltpu.VMEM((nz,) + coded, jnp.int16),
+            pltpu.VMEM((nz,) + coded, jnp.int16),
+            pltpu.VMEM((2, nz - 1, 2) + block, jnp.float32),
+            pltpu.VMEM((nz - 1, 2) + block, jnp.float32),
+            pltpu.VMEM((nz - 1, 2) + coded, jnp.int16),
+            pltpu.VMEM((nz - 1, 2) + coded, jnp.int16),
             dma((4,)),
             dma((2, 2)), dma((2, 2)), dma((2, 2)), dma((2, 2)),
             dma((4 * nz, 2)), dma((4 * nz, 2)), dma((4 * nz, 2)), dma((4 * nz, 2)),
             dma((2, 2)), dma((2, 2)),
-            dma((steps,)), dma((steps,)), dma((steps,)), dma((steps,)),
-            dma((helps,)), dma((helps,)), dma((helps,)), dma((helps,)),
+            dma((nz, 2)), dma((nz, 2)), dma((nz,)), dma((nz,)),
+            dma((nz - 1, 2)), dma((nz - 1, 2)), dma((nz - 1, 2)), dma((nz - 1, 2)),
         ],
         compiler_params=pltpu.CompilerParams(
-            collective_id=0, has_side_effects=True, vmem_limit_bytes=60 * 2**20
+            collective_id=0, has_side_effects=True, vmem_limit_bytes=52 * 2**20
         ),
         cost_estimate=pl.CostEstimate(
             flops=4 * n * rows * nd * k, bytes_accessed=32 * 2**20, transcendentals=0

time: 80.7 us -> 74.6 us (0.924)
  the two profiles are of different devices: /device:TPU:0 before, /device:TPU:1 now
where the time goes in v3:
time: 74.6 us; the launch traced here: 74.4 us
  Pallas kernels  71.4 us (96%)
  other arithmetic  1.83 us (2%)
  local copies, waits for them, and re-layouts  1.23 us (2%)
    pallas_call x1, Pallas kernels, exchange(): pl.pallas_call(functools.partial(kernel, nz), out_shape=jax.ShapeDtypeStr...  71.4 us

profile of v3, /device:TPU:1, one launch (start us, length us, event | category | flops | bytes accessed | tf_op | source)
XLA Modules:
  0.0 74.4 jit_solution(17968512516345520345)
XLA Ops:
  0.0 0.8 %slice_select_fusion = s32[192]{0:T(256)S(1)} fusion(s32[384]{0:T(512)} %param.7, pred[]{:T(512)S(6)} %eq.16), kind=kLoop, calls=%fused_computation.1 | loop fusion | flops 192 | bytes 2305 | tf_op jit(solution)/shard_map/jit(_where)/select_n | solution.py:438
  0.8 0.0 copy-start
  0.8 1.2 %copy-done = bf16[128,1,4096]{2,0,1:T(8,128)(2,1)S(1)} copy-done((bf16[128,1,4096]{2,0,1:T(8,128)(2,1)S(1)}, bf16[128,1,4096]{2,0,1:T(8,128)(2,1)}, u32[]{:S(2)}) %copy-start) | copy-done | bytes 1048600
  2.1 0.0 copy-start.1
  2.1 71.4 %shard_map.46 = f32[192,1024]{1,0:T(8,128)S(1)} custom-call(bf16[128,4096]{1,0:T(8,128)(2,1)S(1)} %bitcast.4, bf16[384,4096]{1,0:T(8,128)(2,1)} %bitcast.5), custom_call_target="tpu_custom_call" | custom-call | flops 3221225472 | bytes 33554432 | tf_op jit(solution)/shard_map/pallas_call | solution.py:392
  73.4 0.0 copy-done.1
  73.4 1.0 %select_bitcast_fusion = f32[1024,192]{0,1:T(8,128)} fusion(f32[192,1024]{1,0:T(8,128)S(1)} %shard_map.46, s32[1024]{0:T(1024)S(1)} %copy-done.1, s32[192]{0:T(256)S(1)} %slice_select_fusion), kind=kLoop, calls=%fused_computation | loop fusion | flops 393216 | bytes 1577728 | tf_op jit(solution)/shard_map/transpose | solution.py:439
Async XLA Ops:
  0.8 1.2 %copy-start = (bf16[128,1,4096]{2,0,1:T(8,128)(2,1)S(1)}, bf16[128,1,4096]{2,0,1:T(8,128)(2,1)}, u32[]{:S(2)}) copy-start(bf16[128,1,4096]{2,0,1:T(8,128)(2,1)} %param.4) | copy-start | bytes 3145732
  2.1 71.4 %copy-start.1 = (s32[1024]{0:T(1024)S(1)}, s32[1024]{0:T(1024)}, u32[]{:S(2)}) copy-start(s32[1024]{0:T(1024)} %param.6) | copy-start | bytes 12292

commit v4 on v3

--- a/solution.py
+++ b/solution.py
@@ -101,13 +101,15 @@
     def chunk(part, zq, sub):
         return (QA, QB)[part].at[zq, sub // 2, pl.ds(pl.multiple_of(sub % 2 * ch, ch), ch)]
 
-    def going_up(i, part):
+    def going_up(i, part, first=False):
         at = chunk(part, z - i // 4, i % 4)
-        return remote(at, at, up_s.at[i, part], up_r.at[i, part], above)
-
-    def going_down(i, part):
+        src = q_ref.at[pl.ds(i * ch, ch), columns(part, True)] if first else at
+        return remote(src, at, up_s.at[i, part], up_r.at[i, part], above)
+
+    def going_down(i, part, first=False):
         at = chunk(part, z + i // 4, i % 4)
-        return remote(at, at, dn_s.at[i, part], dn_r.at[i, part], below)
+        src = q_ref.at[pl.ds(i * ch, ch), columns(part, True)] if first else at
+        return remote(src, at, dn_s.at[i, part], dn_r.at[i, part], below)
 
     def from_below(i, part):
         at = chunk(part, z - 1 - i // 4, i % 4)
@@ -135,11 +137,9 @@
     for h in range(2):
         for part in (1, 0):
             xq(h, part).start()
-    for part in (0, 1):
-        own(part)[0].wait()
-    for h in range(2):
-        send_up(h)
-        send_down(h)
+    for h in range(2):
+        both_parts(lambda part: going_up(h, part, True).start(), has_above, z < nz - 2)
+        both_parts(lambda part: going_down(h, part, True).start(), has_below, z > 1)
     for h in range(2):
         for part in (1, 0):
             xq(h, part).wait_recv()
@@ -149,7 +149,8 @@
         for h in range(2):
             xd(h, part).start()
     for part in (0, 1):
-        own(part)[1].wait()
+        for copy in own(part):
+            copy.wait()
 
     def lend(who, h):
         at = pl.ds(h * nd, nd)
@@ -262,6 +263,7 @@
 
     total = 4 * (nz - 2)
     first = jnp.where(is_end, total, total - 2)
+    early = jnp.where(is_end, nz - 1, 0)
     lax.fori_loop(0, first, relay, 0)
 
     @pl.when(is_helper)
@@ -269,7 +271,6 @@
         for h in range(2):
             lend(1, h).wait_recv()
             help_multiply(1, h, 0, nz - 2)
-        for h in range(2):
             help_add_up(1, h, 0, nz - 2)
 
     @pl.when(~is_end)
@@ -277,22 +278,33 @@
         for h in range(2):
             xd(h, 0).wait_recv()
 
+    lax.fori_loop(first, jnp.maximum(first, total - 1), relay, 0)
     xd(0, 1).wait_recv()
     multiply(1, 0, 0, nz - 1)
     add_up(1, 0, 0, nz - 1)
     for h in range(2):
-        multiply(0, h, 0, nz - 1)
-
-    lax.fori_loop(first, total, relay, 0)
+        multiply(0, h, 0, early)
+
+    @pl.when(is_helper)
+    def _():
+        lend(0, 0).wait_recv()
+        help_multiply(0, 0, 0, nz - 2)
+        help_add_up(0, 0, 0, nz - 2)
+
+    lax.fori_loop(jnp.maximum(first, total - 1), total, relay, 0)
 
     @pl.when(is_helper)
     def _():
         for h in range(2):
             help_multiply(1, h, nz - 2, nz - 1)
+        help_multiply(0, 0, nz - 2, nz - 1)
         for h in range(2):
             help_add_up(1, h, nz - 2, nz - 1)
-        lend(0, 0).wait_recv()
-        help_multiply(0, 0, 0, nz - 1)
+        help_add_up(0, 0, nz - 2, nz - 1)
+
+    xd(1, 1).wait_recv()
+    multiply(1, 1, 0, nz - 1)
+    add_up(1, 1, 0, nz - 1)
 
     @pl.when(z == 0)
     def _():
@@ -304,25 +316,23 @@
         for h in range(4):
             from_below(total + h, 1).wait_recv()
 
-    multiply(1, 0, nz - 1, nz)
-    xd(1, 1).wait_recv()
-    multiply(1, 1, 0, nz)
-
-    @pl.when(is_helper)
-    def _():
-        help_add_up(0, 0, 0, nz - 1)
+    for h in range(2):
+        multiply(1, h, nz - 1, nz)
+
+    @pl.when(is_helper)
+    def _():
         lend(0, 1).wait_recv()
         help_multiply(0, 1, 0, nz - 1)
 
-    add_up(1, 0, nz - 1, nz)
-    add_up(1, 1, 0, nz)
+    for h in range(2):
+        add_up(1, h, nz - 1, nz)
 
     @pl.when(is_helper)
     def _():
         help_add_up(0, 1, 0, nz - 1)
 
     for h in range(2):
-        multiply(0, h, nz - 1, nz)
+        multiply(0, h, early, nz)
     for h in range(2):
         add_up(0, h, 0, nz)
 

time: 74.6 us -> 72 us (0.965)
  the two profiles are of different devices: /device:TPU:1 before, /device:TPU:0 now
where the time goes in v4:
time: 72 us; the launch traced here: 71.8 us
  Pallas kernels  68.8 us (96%)
  other arithmetic  1.83 us (3%)
  local copies, waits for them, and re-layouts  1.23 us (2%)
    pallas_call x1, Pallas kernels, exchange(): pl.pallas_call(functools.partial(kernel, nz), out_shape=jax.ShapeDtypeStr...  68.8 us

profile of v4, /device:TPU:0, one launch (start us, length us, event | category | flops | bytes accessed | tf_op | source)
XLA Modules:
  0.0 71.8 jit_solution(10457997070754731822)
XLA Ops:
  0.0 0.8 %slice_select_fusion = s32[192]{0:T(256)S(1)} fusion(s32[384]{0:T(512)} %param.7, pred[]{:T(512)S(6)} %eq.16), kind=kLoop, calls=%fused_computation.1 | loop fusion | flops 192 | bytes 2305 | tf_op jit(solution)/shard_map/jit(_where)/select_n | solution.py:448
  0.8 0.0 copy-start
  0.8 1.2 %copy-done = bf16[128,1,4096]{2,0,1:T(8,128)(2,1)S(1)} copy-done((bf16[128,1,4096]{2,0,1:T(8,128)(2,1)S(1)}, bf16[128,1,4096]{2,0,1:T(8,128)(2,1)}, u32[]{:S(2)}) %copy-start) | copy-done | bytes 1048600
  2.1 0.0 copy-start.1
  2.1 68.8 %shard_map.46 = f32[192,1024]{1,0:T(8,128)S(1)} custom-call(bf16[128,4096]{1,0:T(8,128)(2,1)S(1)} %bitcast.4, bf16[384,4096]{1,0:T(8,128)(2,1)} %bitcast.5), custom_call_target="tpu_custom_call" | custom-call | flops 3221225472 | bytes 33554432 | tf_op jit(solution)/shard_map/pallas_call | solution.py:402
  70.8 0.0 copy-done.1
  70.8 1.0 %select_bitcast_fusion = f32[1024,192]{0,1:T(8,128)} fusion(f32[192,1024]{1,0:T(8,128)S(1)} %shard_map.46, s32[1024]{0:T(1024)S(1)} %copy-done.1, s32[192]{0:T(256)S(1)} %slice_select_fusion), kind=kLoop, calls=%fused_computation | loop fusion | flops 393216 | bytes 1577728 | tf_op jit(solution)/shard_map/transpose | solution.py:449
Async XLA Ops:
  0.8 1.2 %copy-start = (bf16[128,1,4096]{2,0,1:T(8,128)(2,1)S(1)}, bf16[128,1,4096]{2,0,1:T(8,128)(2,1)}, u32[]{:S(2)}) copy-start(bf16[128,1,4096]{2,0,1:T(8,128)(2,1)} %param.4) | copy-start | bytes 3145732
  2.1 68.8 %copy-start.1 = (s32[1024]{0:T(1024)S(1)}, s32[1024]{0:T(1024)}, u32[]{:S(2)}) copy-start(s32[1024]{0:T(1024)} %param.6) | copy-start | bytes 12292

commit v5 on v4

--- a/solution.py
+++ b/solution.py
@@ -395,7 +395,7 @@
     rows, k = queries.shape
     nd = documents.shape[0] // 2
     nz, half = n // 2, k // 2
-    ka = half // 128 * 3 // 8 * 128
+    ka = half // 128 * 7 // 16 * 128
     kb = half - ka
     block, coded = (nd, 2 * rows), (nd + 16, 2 * rows)
     dma = pltpu.SemaphoreType.DMA

time: 72 us -> 70.5 us (0.979)
  Pallas kernels: 68.8 us -> 67.2 us
    pallas_call x1, Pallas kernels: 68.8 us -> 67.2 us  [exchange(): pl.pallas_call(functools.partial(kernel, nz), out_shape=jax.ShapeDtypeStr...]
where the time goes in v5:
time: 70.5 us; the launch traced here: 70.3 us
  Pallas kernels  67.2 us (95%)
  other arithmetic  1.83 us (3%)
  local copies, waits for them, and re-layouts  1.23 us (2%)
    pallas_call x1, Pallas kernels, exchange(): pl.pallas_call(functools.partial(kernel, nz), out_shape=jax.ShapeDtypeStr...  67.2 us

profile of v5, /device:TPU:0, one launch (start us, length us, event | category | flops | bytes accessed | tf_op | source)
XLA Modules:
  0.0 70.3 jit_solution(4998045065521857292)
XLA Ops:
  0.0 0.8 %slice_select_fusion = s32[192]{0:T(256)S(1)} fusion(s32[384]{0:T(512)} %param.7, pred[]{:T(512)S(6)} %eq.16), kind=kLoop, calls=%fused_computation.1 | loop fusion | flops 192 | bytes 2305 | tf_op jit(solution)/shard_map/jit(_where)/select_n | solution.py:448
  0.8 0.0 copy-start
  0.8 1.2 %copy-done = bf16[128,1,4096]{2,0,1:T(8,128)(2,1)S(1)} copy-done((bf16[128,1,4096]{2,0,1:T(8,128)(2,1)S(1)}, bf16[128,1,4096]{2,0,1:T(8,128)(2,1)}, u32[]{:S(2)}) %copy-start) | copy-done | bytes 1048600
  2.1 0.0 copy-start.1
  2.1 67.2 %shard_map.46 = f32[192,1024]{1,0:T(8,128)S(1)} custom-call(bf16[128,4096]{1,0:T(8,128)(2,1)S(1)} %bitcast.4, bf16[384,4096]{1,0:T(8,128)(2,1)} %bitcast.5), custom_call_target="tpu_custom_call" | custom-call | flops 3221225472 | bytes 33554432 | tf_op jit(solution)/shard_map/pallas_call | solution.py:402
  69.3 0.0 copy-done.1
  69.3 1.0 %select_bitcast_fusion = f32[1024,192]{0,1:T(8,128)} fusion(f32[192,1024]{1,0:T(8,128)S(1)} %shard_map.46, s32[1024]{0:T(1024)S(1)} %copy-done.1, s32[192]{0:T(256)S(1)} %slice_select_fusion), kind=kLoop, calls=%fused_computation | loop fusion | flops 393216 | bytes 1577728 | tf_op jit(solution)/shard_map/transpose | solution.py:449
Async XLA Ops:
  0.8 1.2 %copy-start = (bf16[128,1,4096]{2,0,1:T(8,128)(2,1)S(1)}, bf16[128,1,4096]{2,0,1:T(8,128)(2,1)}, u32[]{:S(2)}) copy-start(bf16[128,1,4096]{2,0,1:T(8,128)(2,1)} %param.4) | copy-start | bytes 3145732
  2.1 67.2 %copy-start.1 = (s32[1024]{0:T(1024)S(1)}, s32[1024]{0:T(1024)}, u32[]{:S(2)}) copy-start(s32[1024]{0:T(1024)} %param.6) | copy-start | bytes 12292
